TPU v7x, 32 devices: a whole 2x2x4 slice. The times are simulated.
32 devices in a mesh: parts: 2 (over y), warp: 4 (over z), weft: 2 (over x), ply: 2 (over core).
Axes of the slice: x: 2, y: 2, z: 4, core: 2. Of those that a mesh axis runs over, the one named last changes fastest.
Arguments:
- lam_start: float32 [64, 256, 512], P(('parts', 'warp', 'ply'), 'weft'), parts along dimension 0, as said below
- resid_start: float32 [64, 256, 512], P(('parts', 'warp', 'ply'), 'weft'), parts along dimension 0, as said below
- dirn_start: float32 [64, 256, 512], P(('parts', 'warp', 'ply'), 'weft'), parts along dimension 0, as said below
- rz_start: float32 [2], P('parts'), parts along dimension 0, may hold values from 10485760 to 83886080
- pattern: int32 [64, 256], P(('parts', 'warp', 'ply'), 'weft'), parts along dimension 0, may hold values from 0 to 2
- corners: int32 [4, 64, 256], P(None, ('parts', 'warp', 'ply'), 'weft'), parts along dimension 1, may hold values from -1 to 127, as said below
- schur_inv: float32 [3, 512, 512], replicated, as said below
- schur_dirichlet: float32 [3, 512, 512], replicated, as said below
- corner_shape: float32 [3, 4, 512], replicated, may hold values from -0.3 to 0.3
- coarse_inv: float32 [256, 128], P(('parts', 'warp', 'weft', 'ply')), parts along dimension 0, as said below
Outputs:
- lam_final: float32 [64, 256, 512], P(('parts', 'warp', 'ply'), 'weft'), parts along dimension 0
- resid_final: float32 [64, 256, 512], P(('parts', 'warp', 'ply'), 'weft'), parts along dimension 0
- dirn_final: float32 [64, 256, 512], P(('parts', 'warp', 'ply'), 'weft'), parts along dimension 0
There are 2 independent parts, one for each index of `parts`. A program takes and returns all parts, laid end to end along the dimension named above; an argument that names none is the same for every part. Nothing has to cross between parts.
Inputs may be any that keep to these rules, and one draw needn't show every extreme that they name: `lam_start`: in each cell the W block is minus the E block of the cell to its west and zero where j = 0; the S block is minus the N block of the cell to its south and zero where i = 0. `resid_start`: in each cell the W block is minus the E block of the cell to its west and zero where j = 0; the S block is minus the N block of the cell to its south and zero where i = 0. `dirn_start`: in each cell the W block is minus the E block of the cell to its west and zero where j = 0; the S block is minus the N block of the cell to its south and zero where i = 0. `corners`: corner k of cell (i, j) is the corner node (i, j), (i, j + 1), (i + 1, j) or (i + 1, j + 1) for k = 0, 1, 2, 3; nodes (a, b) with a = 32 or b = 256 are -1; every other node's row is that of its aggregate, the block of 8 x 8 nodes with the same a // 8 and b // 8; each aggregate has its own row, and which aggregate has which row is drawn. `schur_inv`: each matrix is symmetric positive definite. `schur_dirichlet`: each matrix is symmetric positive definite. `coarse_inv`: symmetric positive definite.
All inputs are finite; a program needn't handle non-finite values.
Results may differ from a plain program's by a relative error of at most 0.00027.
Values sent between devices are 32-bit elements; how exact they have to be, the bound alone decides.
A program may use at most 64 MiB of HBM per device.

v0:
```python
import jax
import jax.numpy as jnp
from jax import lax
from jax.sharding import PartitionSpec as P

ITERS = 3
HIGHEST = lax.Precision.HIGHEST


def with_halo(array, sides, width):
    for axis, dim in sides:
        count, length = (lax.axis_size(axis), array.shape[dim])
        up = [(i, (i + 1) % count) for i in range(count - 1)]
        down = [(j, i) for i, j in up]
        last = lax.slice_in_dim(array, length - width, length, axis=dim)
        leading = lax.slice_in_dim(array, 0, width, axis=dim)
        before = lax.ppermute(last, axis, up)
        after = lax.ppermute(leading, axis, down)
        array = jnp.concatenate([before, array, after], axis=dim)
    return array


def split_edges(values, edge_len):
    return (
        values[..., :edge_len],
        values[..., edge_len : 2 * edge_len],
        values[..., 2 * edge_len : 3 * edge_len],
        values[..., 3 * edge_len :],
    )


def cross_faces(values, edge_len, west_keep, south_keep):
    west_side, east_side, south_side, north_side = split_edges(values, edge_len)
    rows_here, cols_here = (values.shape[0], values.shape[1])
    local_row = lax.broadcasted_iota(jnp.int32, (rows_here, cols_here, 1), 0)
    local_col = lax.broadcasted_iota(jnp.int32, (rows_here, cols_here, 1), 1)
    along_rows = jnp.where(local_row == 0, south_side, north_side)
    along_cols = jnp.where(local_col == 0, west_side, east_side)
    padded = with_halo(
        jnp.concatenate([along_rows, along_cols], axis=2), ((("warp", "ply"), 0), ("weft", 1)), 1
    )
    from_south = padded[0, 1:-1, :edge_len]
    from_north = padded[-1, 1:-1, :edge_len]
    from_west = padded[1:-1, 0, edge_len:]
    from_east = padded[1:-1, -1, edge_len:]
    east_west = jnp.concatenate([west_side[:, 1:], from_east[:, None]], axis=1)
    west_east = jnp.concatenate([from_west[:, None], east_side[:, :-1]], axis=1)
    north_south = jnp.concatenate([south_side[1:], from_north[None]], axis=0)
    south_north = jnp.concatenate([from_south[None], north_side[:-1]], axis=0)
    return jnp.concatenate(
        [
            (west_side - west_east) * west_keep,
            east_side - east_west,
            (south_side - south_north) * south_keep,
            north_side - north_south,
        ],
        axis=2,
    )


def apply_cells(rows_flat, matrices, cell_order, inverse, group_sizes):
    sorted_rows = rows_flat[cell_order]
    product = lax.ragged_dot(
        sorted_rows, matrices, group_sizes, precision=HIGHEST, preferred_element_type=jnp.float32
    )
    return product[inverse]


def on_device(
    lam_start,
    resid_start,
    dirn_start,
    rz_start,
    pattern,
    corners,
    schur_inv,
    schur_dirichlet,
    corner_shape,
    coarse_inv,
):
    rows_here, cols_here, dof_count = lam_start.shape
    edge_len = dof_count // 4
    pattern_count = schur_inv.shape[0]
    coarse_count = coarse_inv.shape[1]
    row_pos = (
        lax.broadcasted_iota(jnp.int32, (rows_here, cols_here, 1), 0)
        + lax.axis_index(("warp", "ply")) * rows_here
    )
    col_pos = (
        lax.broadcasted_iota(jnp.int32, (rows_here, cols_here, 1), 1)
        + lax.axis_index("weft") * cols_here
    )
    total_rows = lax.axis_size(("warp", "ply")) * rows_here
    total_cols = lax.axis_size("weft") * cols_here
    west_keep = (col_pos > 0).astype(jnp.float32)
    south_keep = (row_pos > 0).astype(jnp.float32)
    east_weight = jnp.where(col_pos == total_cols - 1, 1.0, 0.5).astype(jnp.float32)
    north_weight = jnp.where(row_pos == total_rows - 1, 1.0, 0.5).astype(jnp.float32)
    block_shape = (rows_here, cols_here, edge_len)
    edge_weight = jnp.concatenate(
        [
            jnp.broadcast_to(0.5 * west_keep, block_shape),
            jnp.broadcast_to(east_weight, block_shape),
            jnp.broadcast_to(0.5 * south_keep, block_shape),
            jnp.broadcast_to(north_weight, block_shape),
        ],
        axis=2,
    )
    cell_kind = pattern.reshape(-1)
    cell_order = jnp.argsort(cell_kind, stable=True)
    inverse = jnp.argsort(cell_order, stable=True)
    selector = (cell_kind[None, :] == jnp.arange(pattern_count, dtype=jnp.int32)[:, None]).astype(
        jnp.float32
    )
    group_sizes = jnp.sum(selector, axis=1).astype(jnp.int32)
    corner_rows = corners.reshape(4, -1)
    corner_live = corner_rows >= 0
    corner_slot = jnp.where(corner_live, corner_rows, coarse_count)
    corner_pick = jnp.where(corner_live, corner_rows, 0)
    multiplier, residual, direction = (lam_start, resid_start, dirn_start)
    rz_prev = rz_start[0]
    for iteration in range(ITERS):
        scaled = (edge_weight * residual).reshape(-1, dof_count)
        spread = apply_cells(scaled, schur_dirichlet, cell_order, inverse, group_sizes).reshape(
            residual.shape
        )
        precond = edge_weight * cross_faces(spread, edge_len, west_keep, south_keep)
        rz_now = lax.psum(jnp.sum(edge_weight * residual * precond), ("warp", "weft", "ply"))
        direction = precond + rz_now / rz_prev * direction
        rows_flat = direction.reshape(-1, dof_count)
        local_image = apply_cells(rows_flat, schur_inv, cell_order, inverse, group_sizes)
        corner_terms = jnp.einsum("pkd,cd->pkc", corner_shape, rows_flat, precision=HIGHEST)
        corner_load = jnp.sum(corner_terms * selector[:, None, :], axis=0)
        partial_rhs = jax.ops.segment_sum(
            corner_load.reshape(-1), corner_slot.reshape(-1), num_segments=coarse_count + 1
        )[:coarse_count]
        coarse_rhs = lax.psum(partial_rhs, ("warp", "weft", "ply"))
        coarse_sol = lax.all_gather(
            jnp.dot(coarse_inv, coarse_rhs, precision=HIGHEST),
            ("warp", "weft", "ply"),
            axis=0,
            tiled=True,
        )
        corner_vals = jnp.where(corner_live, coarse_sol[corner_pick], 0.0)
        full_image = local_image + jnp.einsum(
            "pkc,pkd->cd", selector[:, None, :] * corner_vals[None], corner_shape, precision=HIGHEST
        )
        applied = cross_faces(full_image.reshape(direction.shape), edge_len, west_keep, south_keep)
        curvature = lax.psum(jnp.sum(edge_weight * direction * applied), ("warp", "weft", "ply"))
        alpha_step = rz_now / curvature
        multiplier = multiplier + alpha_step * direction
        residual = residual - alpha_step * applied
        rz_prev = rz_now
    return (multiplier, residual, direction)


def solution(mesh):
    return jax.shard_map(
        on_device,
        mesh=mesh,
        in_specs=(
            P(("parts", "warp", "ply"), "weft", None),
            P(("parts", "warp", "ply"), "weft", None),
            P(("parts", "warp", "ply"), "weft", None),
            P("parts"),
            P(("parts", "warp", "ply"), "weft"),
            P(None, ("parts", "warp", "ply"), "weft"),
            P(),
            P(),
            P(),
            P(("parts", "warp", "weft", "ply"), None),
        ),
        out_specs=(
            P(("parts", "warp", "ply"), "weft", None),
            P(("parts", "warp", "ply"), "weft", None),
            P(("parts", "warp", "ply"), "weft", None),
        ),
        check_vma=False,
    )
```

profile of v0, /device:TPU:0, one launch (start us, length us, event | category | flops | bytes accessed | tf_op | source)
XLA Modules:
  0.0 678.7 jit_solution(7160559662432840204)
XLA Ops:
  3.4 4.4 sort.31
  7.8 3.8 sort.32
  13.5 2.3 gather_fusion
  15.8 8.7 %ragged-dot-none.5 = f32[512,512]{1,0:T(8,128)} custom-call(s32[1]{0:T(128)} %get-tuple-element.27, s32[4]{0:T(128)} %get-tuple-element.28, s32[4]{0:T(128)} %get-tuple-element.29, s32[4]{0:T(128)} %get-tuple-element.30, s32[1]{0:T(128)} %get-tuple-element.27, f32[512,512]{1,0:T(8,128)} %gather_fusion, f32[3,512,512]{2,1,0:T(8,128)} %param.17), custom_call_target="tpu_custom_call" | custom-call | flops 268435456 | bytes 5242892 | tf_op jit(solution)/shard_map/ragged_dot_general/ragged-dot-none
  24.6 3.3 gather_fusion.1
  29.4 3.1 collective-permute-start
  38.5 3.4 collective-permute-start.2
  50.5 33.6 %psum.63 = f32[]{:T(128)} all-reduce(f32[]{:T(128)} %multiply_reduce_fusion.2), channel_id=1, replica_groups=mesh['parts'=2,'warp'=4,'weft'=2,'ply'=2] {'warp','weft','ply'}, use_global_device_ids=true, to_apply=%region_4.5 | all-reduce | flops 1 | bytes 8 | tf_op jit(solution)/shard_map/psum | solution.py:128
  87.2 14.7 %scatter_custom_fusion = f32[129]{0:T(256)S(1)} fusion(s32[2048]{0:T(1024)S(1)} %bitcast.138, f32[2048]{0:T(1024)S(1)} %bitcast.142, f32[]{:T(128)} %constant.17.clone.1), kind=kCustom, calls=%fused_computation.187 | custom fusion | flops 2048 | bytes 520 | tf_op jit(solution)/shard_map/scatter-add | solution.py:134
  101.8 29.5 %psum.64 = f32[128]{0:T(128)S(1)} all-reduce(f32[128]{0:T(128)S(1)} %slice.337), channel_id=1, replica_groups=mesh['parts'=2,'warp'=4,'weft'=2,'ply'=2] {'warp','weft','ply'}, use_global_device_ids=true, to_apply=%region_7.8 | all-reduce | flops 128 | bytes 1024 | tf_op jit(solution)/shard_map/psum | solution.py:137
  131.7 29.5 %all-reduce = f32[128]{0:T(128)S(1)} all-reduce(f32[128]{0:T(128)S(1)} %dynamic-update-slice), channel_id=1, replica_groups=mesh['parts'=2,'warp'=4,'weft'=2,'ply'=2] {'warp','weft','ply'}, use_global_device_ids=true, to_apply=%add | all-reduce | flops 128 | bytes 1024
  161.1 12.6 %gather_fusion.4 = f32[2048]{0:T(1024)S(1)} fusion(f32[128]{0:T(128)S(1)} %all-reduce, s32[2048]{0:T(1024)S(1)} %broadcast_clamp_fusion), kind=kCustom, calls=%fused_computation.4 | custom fusion | bytes 24576 | tf_op jit(solution)/shard_map/gather | solution.py:144
  173.8 2.3 gather_fusion.2
  176.1 8.7 %ragged-dot-none.4 = f32[512,512]{1,0:T(8,128)} custom-call(s32[1]{0:T(128)} %get-tuple-element.27, s32[4]{0:T(128)} %get-tuple-element.28, s32[4]{0:T(128)} %get-tuple-element.29, s32[4]{0:T(128)} %get-tuple-element.30, s32[1]{0:T(128)} %get-tuple-element.27, f32[512,512]{1,0:T(8,128)} %gather_fusion.2, f32[3,512,512]{2,1,0:T(8,128)} %param.16), custom_call_target="tpu_custom_call" | custom-call | flops 268435456 | bytes 5242892 | tf_op jit(solution)/shard_map/ragged_dot_general/ragged-dot-none
  184.8 3.9 gather_fusion.3
  188.8 2.3 fusion
  199.1 4.0 collective-permute-done.7
  205.1 32.0 %psum.65 = f32[]{:T(128)} all-reduce(f32[]{:T(128)} %fusion.23), channel_id=1, replica_groups=mesh['parts'=2,'warp'=4,'weft'=2,'ply'=2] {'warp','weft','ply'}, use_global_device_ids=true, to_apply=%region_9.10 | all-reduce | flops 1 | bytes 8 | tf_op jit(solution)/shard_map/psum | solution.py:149
  240.1 2.3 gather_fusion.5
  242.4 8.7 %ragged-dot-none.3 = f32[512,512]{1,0:T(8,128)} custom-call(s32[1]{0:T(128)} %get-tuple-element.27, s32[4]{0:T(128)} %get-tuple-element.28, s32[4]{0:T(128)} %get-tuple-element.29, s32[4]{0:T(128)} %get-tuple-element.30, s32[1]{0:T(128)} %get-tuple-element.27, f32[512,512]{1,0:T(8,128)} %gather_fusion.5, f32[3,512,512]{2,1,0:T(8,128)} %param.17), custom_call_target="tpu_custom_call" | custom-call | flops 268435456 | bytes 5242892 | tf_op jit(solution)/shard_map/ragged_dot_general/ragged-dot-none
  251.2 3.9 gather_fusion.6
  263.8 4.1 collective-permute-done.11
  270.0 30.6 %psum.66 = f32[]{:T(128)} all-reduce(f32[]{:T(128)} %multiply_reduce_fusion.1), channel_id=1, replica_groups=mesh['parts'=2,'warp'=4,'weft'=2,'ply'=2] {'warp','weft','ply'}, use_global_device_ids=true, to_apply=%region_11.12 | all-reduce | flops 1 | bytes 8 | tf_op jit(solution)/shard_map/psum | solution.py:128
  304.3 14.7 %scatter_custom_fusion.1 = f32[129]{0:T(256)S(1)} fusion(s32[2048]{0:T(1024)S(1)} %bitcast.139, f32[2048]{0:T(1024)S(1)} %bitcast.143, f32[]{:T(128)} %constant.17.clone.1), kind=kCustom, calls=%fused_computation.185 | custom fusion | flops 2048 | bytes 520 | tf_op jit(solution)/shard_map/scatter-add | solution.py:134
  319.0 29.5 %psum.67 = f32[128]{0:T(128)S(1)} all-reduce(f32[128]{0:T(128)S(1)} %slice.370), channel_id=1, replica_groups=mesh['parts'=2,'warp'=4,'weft'=2,'ply'=2] {'warp','weft','ply'}, use_global_device_ids=true, to_apply=%region_14.15 | all-reduce | flops 128 | bytes 1024 | tf_op jit(solution)/shard_map/psum | solution.py:137
  348.8 29.5 %all-reduce.1 = f32[128]{0:T(128)S(1)} all-reduce(f32[128]{0:T(128)S(1)} %dynamic-update-slice.1), channel_id=1, replica_groups=mesh['parts'=2,'warp'=4,'weft'=2,'ply'=2] {'warp','weft','ply'}, use_global_device_ids=true, to_apply=%add.1 | all-reduce | flops 128 | bytes 1024
  378.3 12.6 %gather_fusion.9 = f32[2048]{0:T(1024)S(1)} fusion(f32[128]{0:T(128)S(1)} %all-reduce.1, s32[2048]{0:T(1024)S(1)} %broadcast_clamp_fusion), kind=kCustom, calls=%fused_computation.9 | custom fusion | bytes 24576 | tf_op jit(solution)/shard_map/gather | solution.py:144
  391.0 2.3 gather_fusion.7
  393.3 8.7 %ragged-dot-none.2 = f32[512,512]{1,0:T(8,128)} custom-call(s32[1]{0:T(128)} %get-tuple-element.27, s32[4]{0:T(128)} %get-tuple-element.28, s32[4]{0:T(128)} %get-tuple-element.29, s32[4]{0:T(128)} %get-tuple-element.30, s32[1]{0:T(128)} %get-tuple-element.27, f32[512,512]{1,0:T(8,128)} %gather_fusion.7, f32[3,512,512]{2,1,0:T(8,128)} %param.16), custom_call_target="tpu_custom_call" | custom-call | flops 268435456 | bytes 5242892 | tf_op jit(solution)/shard_map/ragged_dot_general/ragged-dot-none
  402.0 3.9 gather_fusion.8
  416.1 4.1 collective-permute-done.15
  422.3 32.2 %psum.68 = f32[]{:T(128)} all-reduce(f32[]{:T(128)} %fusion.22), channel_id=1, replica_groups=mesh['parts'=2,'warp'=4,'weft'=2,'ply'=2] {'warp','weft','ply'}, use_global_device_ids=true, to_apply=%region_16.17 | all-reduce | flops 1 | bytes 8 | tf_op jit(solution)/shard_map/psum | solution.py:149
  455.9 3.4 fusion.11
  459.2 2.3 gather_fusion.10
  461.6 8.7 %ragged-dot-none.1 = f32[512,512]{1,0:T(8,128)} custom-call(s32[1]{0:T(128)} %get-tuple-element.27, s32[4]{0:T(128)} %get-tuple-element.28, s32[4]{0:T(128)} %get-tuple-element.29, s32[4]{0:T(128)} %get-tuple-element.30, s32[1]{0:T(128)} %get-tuple-element.27, f32[512,512]{1,0:T(8,128)} %gather_fusion.10, f32[3,512,512]{2,1,0:T(8,128)} %param.17), custom_call_target="tpu_custom_call" | custom-call | flops 268435456 | bytes 5242892 | tf_op jit(solution)/shard_map/ragged_dot_general/ragged-dot-none
  470.3 3.2 gather_fusion.11
  483.1 3.1 collective-permute-done.19
  488.3 30.6 %psum.69 = f32[]{:T(128)} all-reduce(f32[]{:T(128)} %multiply_reduce_fusion), channel_id=1, replica_groups=mesh['parts'=2,'warp'=4,'weft'=2,'ply'=2] {'warp','weft','ply'}, use_global_device_ids=true, to_apply=%region_18.19 | all-reduce | flops 1 | bytes 8 | tf_op jit(solution)/shard_map/psum | solution.py:128
  522.9 14.7 %scatter_custom_fusion.2 = f32[129]{0:T(256)S(1)} fusion(s32[2048]{0:T(1024)S(1)} %bitcast.140, f32[2048]{0:T(1024)S(1)} %bitcast.141, f32[]{:T(128)} %constant.17.clone.1), kind=kCustom, calls=%fused_computation.183 | custom fusion | flops 2048 | bytes 520 | tf_op jit(solution)/shard_map/scatter-add | solution.py:134
  537.5 29.5 %psum.70 = f32[128]{0:T(128)S(1)} all-reduce(f32[128]{0:T(128)S(1)} %slice.403), channel_id=1, replica_groups=mesh['parts'=2,'warp'=4,'weft'=2,'ply'=2] {'warp','weft','ply'}, use_global_device_ids=true, to_apply=%region_21.22 | all-reduce | flops 128 | bytes 1024 | tf_op jit(solution)/shard_map/psum | solution.py:137
  567.4 29.5 %all-reduce.2 = f32[128]{0:T(128)S(1)} all-reduce(f32[128]{0:T(128)S(1)} %dynamic-update-slice.2), channel_id=1, replica_groups=mesh['parts'=2,'warp'=4,'weft'=2,'ply'=2] {'warp','weft','ply'}, use_global_device_ids=true, to_apply=%add.2 | all-reduce | flops 128 | bytes 1024
  596.8 12.6 %gather_fusion.14 = f32[2048]{0:T(1024)S(1)} fusion(f32[128]{0:T(128)S(1)} %all-reduce.2, s32[2048]{0:T(1024)S(1)} %broadcast_clamp_fusion), kind=kCustom, calls=%fused_computation.14 | custom fusion | bytes 24576 | tf_op jit(solution)/shard_map/gather | solution.py:144
  609.5 2.3 gather_fusion.12
  611.8 8.8 %ragged-dot-none = f32[512,512]{1,0:T(8,128)} custom-call(s32[1]{0:T(128)} %get-tuple-element.27, s32[4]{0:T(128)} %get-tuple-element.28, s32[4]{0:T(128)} %get-tuple-element.29, s32[4]{0:T(128)} %get-tuple-element.30, s32[1]{0:T(128)} %get-tuple-element.27, f32[512,512]{1,0:T(8,128)} %gather_fusion.12, f32[3,512,512]{2,1,0:T(8,128)} %param.16), custom_call_target="tpu_custom_call" | custom-call | flops 268435456 | bytes 5242892 | tf_op jit(solution)/shard_map/ragged_dot_general/ragged-dot-none
  620.6 3.9 gather_fusion.13
  634.8 4.1 collective-permute-done.23
  641.1 32.1 %psum.71 = f32[]{:T(128)} all-reduce(f32[]{:T(128)} %fusion.21), channel_id=1, replica_groups=mesh['parts'=2,'warp'=4,'weft'=2,'ply'=2] {'warp','weft','ply'}, use_global_device_ids=true, to_apply=%region_23.24 | all-reduce | flops 1 | bytes 8 | tf_op jit(solution)/shard_map/psum | solution.py:149
  674.4 2.7 multiply_subtract_fusion
  (256 shorter events, 87.2 us)
Async XLA Ops:
  0.6 85.5 %copy-start = (f32[3,4,512]{2,1,0:T(4,128)S(1)}, f32[3,4,512]{2,1,0:T(4,128)}, u32[]{:S(2)}) copy-start(f32[3,4,512]{2,1,0:T(4,128)} %param.18) | copy-start | bytes 73732
  11.8 408.7 %copy-start.2 = (f32[4,128,128]{2,1,0:T(8,128)}, f32[4,128,128]{2,1,0:T(8,128)S(1)}, u32[]{:S(2)}) copy-start(f32[4,128,128]{2,1,0:T(8,128)S(1)} %broadcast_in_dim.140) | copy-start | bytes 786436
  11.9 408.6 %copy-start.5 = (f32[4,128,128]{2,1,0:T(8,128)}, f32[4,128,128]{2,1,0:T(8,128)S(1)}, u32[]{:S(2)}) copy-start(f32[4,128,128]{2,1,0:T(8,128)S(1)} %broadcast_in_dim.135) | copy-start | bytes 786436
  12.0 408.5 %copy-start.8 = (f32[4,128,128]{2,1,0:T(8,128)}, f32[4,128,128]{2,1,0:T(8,128)S(1)}, u32[]{:S(2)}) copy-start(f32[4,128,128]{2,1,0:T(8,128)S(1)} %broadcast_in_dim.138) | copy-start | bytes 786436
  24.6 9.3 %copy-start.41 = (s32[4,4,128]{2,1,0:T(4,128)S(1)}, s32[4,4,128]{2,1,0:T(4,128)}, u32[]{:S(2)}) copy-start(s32[4,4,128]{2,1,0:T(4,128)} %param.15) | copy-start | bytes 24580
  27.8 7.7 %copy-start.43 = (s32[4,128]{1,0:T(4,128)S(1)}, s32[4,128]{1,0:T(4,128)}, u32[]{:S(2)}) copy-start(s32[4,128]{1,0:T(4,128)} %param.14) | copy-start | bytes 6148
  27.9 16.0 %copy-start.44 = (u32[32]{0:T(128)S(1)}, u32[32]{0:T(128)}, u32[]{:S(2)}) copy-start(u32[32]{0:T(128)} %constant.48) | copy-start | bytes 388
  29.4 19.4 %copy-start.11 = (f32[4,128,512]{2,1,0:T(8,128)S(1)}, f32[4,128,512]{2,1,0:T(8,128)}, u32[]{:S(2)}) copy-start(f32[4,128,512]{2,1,0:T(8,128)} %param.11) | copy-start | bytes 3145732
  29.4 6.2 collective-permute-start
  32.6 5.1 collective-permute-start.1
  38.5 7.7 %collective-permute-start.2 = (f32[6,1,256]{2,1,0:T(1,128)S(1)}, f32[6,1,256]{2,1,0:T(1,128)S(1)}, u32[]{:S(2)}, u32[]{:S(2)}) collective-permute-start(f32[6,1,256]{2,1,0:T(1,128)S(1)} %get-tuple-element.103), channel_id=1, source_target_pairs={{0,2},{1,3},{4,6},{5,7},{8,10},{9,11},{12,14},{13,15},{16,18},{17,... | collective-permute-start | bytes 18440 | tf_op jit(solution)/shard_map/ppermute | solution.py:17
  41.9 5.5 collective-permute-start.3
  48.8 35.8 %copy-start.39 = (f32[4,128,512]{2,1,0:T(8,128)S(1)}, f32[4,128,512]{2,1,0:T(8,128)}, u32[]{:S(2)}) copy-start(f32[4,128,512]{2,1,0:T(8,128)} %param.12) | copy-start | bytes 3145732
  49.8 81.5 %copy-start.42 = (f32[8,128]{1,0:T(8,128)S(1)}, f32[8,128]{1,0:T(8,128)}, u32[]{:S(2)}) copy-start(f32[8,128]{1,0:T(8,128)} %param.19) | copy-start | bytes 12292
  191.2 3.1 collective-permute-start.4
  193.0 3.2 collective-permute-start.5
  196.3 2.8 collective-permute-start.6
  197.6 5.5 collective-permute-start.7
  203.3 36.7 %copy-start.16 = (f32[4,128,128]{2,1,0:T(8,128)}, f32[4,128,128]{2,1,0:T(8,128)S(1)}, u32[]{:S(2)}) copy-start(f32[4,128,128]{2,1,0:T(8,128)S(1)} %get-tuple-element.73) | copy-start | bytes 786436
  255.1 8.6 %copy-start.12 = (f32[512,512]{1,0:T(8,128)S(1)}, f32[512,512]{1,0:T(8,128)}, u32[]{:S(2)}) copy-start(f32[512,512]{1,0:T(8,128)} %gather_fusion.6) | copy-start | bytes 3145732
  256.5 3.7 collective-permute-start.8
  257.8 3.2 collective-permute-start.9
  261.1 2.7 collective-permute-start.10
  262.4 5.5 collective-permute-start.11
  408.4 3.1 collective-permute-start.12
  410.2 3.2 collective-permute-start.13
  413.5 2.7 collective-permute-start.14
  414.8 5.5 collective-permute-start.15
  420.5 34.0 %copy-start.35 = (f32[4,128,128]{2,1,0:T(8,128)}, f32[4,128,128]{2,1,0:T(8,128)S(1)}, u32[]{:S(2)}) copy-start(f32[4,128,128]{2,1,0:T(8,128)S(1)} %get-tuple-element.53) | copy-start | bytes 786436
  474.6 11.7 %copy-start.14 = (f32[512,512]{1,0:T(8,128)S(1)}, f32[512,512]{1,0:T(8,128)}, u32[]{:S(2)}) copy-start(f32[512,512]{1,0:T(8,128)} %copy-done.13) | copy-start | bytes 3145732
  474.6 12.8 %copy-start.3 = (f32[4,128,128]{2,1,0:T(8,128)S(1)}, f32[4,128,128]{2,1,0:T(8,128)}, u32[]{:S(2)}) copy-start(f32[4,128,128]{2,1,0:T(8,128)} %copy-done.2) | copy-start | bytes 786436
  474.6 12.7 %copy-start.6 = (f32[4,128,128]{2,1,0:T(8,128)S(1)}, f32[4,128,128]{2,1,0:T(8,128)}, u32[]{:S(2)}) copy-start(f32[4,128,128]{2,1,0:T(8,128)} %copy-done.5) | copy-start | bytes 786436
  474.6 12.7 %copy-start.9 = (f32[4,128,128]{2,1,0:T(8,128)S(1)}, f32[4,128,128]{2,1,0:T(8,128)}, u32[]{:S(2)}) copy-start(f32[4,128,128]{2,1,0:T(8,128)} %copy-done.8) | copy-start | bytes 786436
  474.6 12.7 %copy-start.15 = (f32[4,128,512]{2,1,0:T(8,128)S(1)}, f32[4,128,512]{2,1,0:T(8,128)}, u32[]{:S(2)}) copy-start(f32[4,128,512]{2,1,0:T(8,128)} %get-tuple-element.32) | copy-start | bytes 3145732
  474.6 3.9 collective-permute-start.16
  476.2 3.2 collective-permute-start.17
  479.4 3.7 collective-permute-start.18
  480.7 5.5 collective-permute-start.19
  486.5 32.4 %copy-start.27 = (f32[4,128,128]{2,1,0:T(8,128)}, f32[4,128,128]{2,1,0:T(8,128)S(1)}, u32[]{:S(2)}) copy-start(f32[4,128,128]{2,1,0:T(8,128)S(1)} %get-tuple-element.43) | copy-start | bytes 786436
  521.8 155.4 %copy-start.1 = (f32[4,128,512]{2,1,0:T(8,128)}, f32[4,128,512]{2,1,0:T(8,128)S(1)}, u32[]{:S(2)}) copy-start(f32[4,128,512]{2,1,0:T(8,128)S(1)} %multiply_add_fusion.1) | copy-start | bytes 3145732
  626.9 13.2 %copy-start.4 = (f32[4,128,128]{2,1,0:T(8,128)S(1)}, f32[4,128,128]{2,1,0:T(8,128)}, u32[]{:S(2)}) copy-start(f32[4,128,128]{2,1,0:T(8,128)} %copy-done.2) | copy-start | bytes 786436
  627.0 13.2 %copy-start.7 = (f32[4,128,128]{2,1,0:T(8,128)S(1)}, f32[4,128,128]{2,1,0:T(8,128)}, u32[]{:S(2)}) copy-start(f32[4,128,128]{2,1,0:T(8,128)} %copy-done.5) | copy-start | bytes 786436
  627.0 13.2 %copy-start.10 = (f32[4,128,128]{2,1,0:T(8,128)S(1)}, f32[4,128,128]{2,1,0:T(8,128)}, u32[]{:S(2)}) copy-start(f32[4,128,128]{2,1,0:T(8,128)} %copy-done.8) | copy-start | bytes 786436
  627.0 3.3 collective-permute-start.20
  628.9 3.2 collective-permute-start.21
  632.1 2.7 collective-permute-start.22
  633.4 5.5 collective-permute-start.23
  674.4 2.8 copy-start.40
  (21 other events, 17.3 us)
where the time goes:
time: 681 us; the launch traced here: 679 us
  blocking collectives  368 us (54%)
  local copies, waits for them, and re-layouts  88.5 us (13%)
  other arithmetic  80.7 us (12%)
  Pallas kernels  53.8 us (8%)
  starting transfers between devices  37 us (5%)
  waiting for transfers between devices  30.1 us (4%)
  matrix products  10.3 us (2%)
  between operations  10.3 us (2%)
    psum x3, blocking collectives, on_device(): lax.psum(jnp.sum(edge_weight * direction * applied), ('warp', 'weft', 'pl...  96.3 us
    psum x3, blocking collectives, on_device(): lax.psum(jnp.sum(edge_weight * residual * precond), ('warp', 'weft', 'ply'))  94.8 us
    psum x3, blocking collectives, on_device(): coarse_rhs = lax.psum(partial_rhs, ('warp', 'weft', 'ply'))  88.5 us
    unnamed x3, blocking collectives  88.4 us
    another operation x6, Pallas kernels  52.5 us
    scatter-add x3, other arithmetic, on_device(): jax.ops.segment_sum(corner_load.reshape(-1), corner_slot.reshape(-1), num...  44 us
    gather x6, local copies, waits for them, and re-layouts, on_device(): corner_vals = jnp.where(corner_live, coarse_sol[corner_pick], 0.0)  37.9 us
    ppermute x12, waiting for transfers between devices, with_halo(): after = lax.ppermute(leading, axis, down)  30.1 us
  transfers between devices with their start and end apart: 24, of which 12 were waited for; matrix products, arithmetic and copies ran while one was open for 1% of the time, Pallas kernels for 0%

commit v1 on v0

--- a/solution.py
+++ b/solution.py
@@ -134,7 +134,7 @@
         partial_rhs = jax.ops.segment_sum(
             corner_load.reshape(-1), corner_slot.reshape(-1), num_segments=coarse_count + 1
         )[:coarse_count]
-        coarse_rhs = lax.psum(partial_rhs, ("warp", "weft", "ply"))
+        coarse_rhs = lax.psum(lax.psum(partial_rhs, ("weft", "ply")), "warp")
         coarse_sol = lax.all_gather(
             jnp.dot(coarse_inv, coarse_rhs, precision=HIGHEST),
             ("warp", "weft", "ply"),

time: 681 us -> 635 us (0.932)
  blocking collectives: 368 us -> 322 us
    psum x3 -> x6, blocking collectives: 88.5 us -> 42.3 us  [on_device(): coarse_rhs = lax.psum(lax.psum(partial_rhs, ('weft', 'ply')), 'warp')]
where the time goes in v1:
time: 635 us; the launch traced here: 633 us
  blocking collectives  322 us (51%)
  local copies, waits for them, and re-layouts  88.4 us (14%)
  other arithmetic  80.8 us (13%)
  Pallas kernels  53.7 us (8%)
  starting transfers between devices  37 us (6%)
  waiting for transfers between devices  30.3 us (5%)
  between operations  10.5 us (2%)
  matrix products  10.3 us (2%)
    psum x3, blocking collectives, on_device(): lax.psum(jnp.sum(edge_weight * direction * applied), ('warp', 'weft', 'pl...  96.3 us
    psum x3, blocking collectives, on_device(): lax.psum(jnp.sum(edge_weight * residual * precond), ('warp', 'weft', 'ply'))  94.8 us
    unnamed x3, blocking collectives  88.4 us
    another operation x6, Pallas kernels  52.4 us
    scatter-add x3, other arithmetic, on_device(): jax.ops.segment_sum(corner_load.reshape(-1), corner_slot.reshape(-1), num...  44 us
    psum x6, blocking collectives, on_device(): coarse_rhs = lax.psum(lax.psum(partial_rhs, ('weft', 'ply')), 'warp')  42.3 us
    gather x6, local copies, waits for them, and re-layouts, on_device(): corner_vals = jnp.where(corner_live, coarse_sol[corner_pick], 0.0)  37.9 us
    ppermute x12, waiting for transfers between devices, with_halo(): after = lax.ppermute(leading, axis, down)  30.2 us
  transfers between devices with their start and end apart: 24, of which 12 were waited for; matrix products, arithmetic and copies ran while one was open for 1% of the time, Pallas kernels for 0%

profile of v1, /device:TPU:0, one launch (start us, length us, event | category | flops | bytes accessed | tf_op | source)
XLA Modules:
  0.0 632.8 jit_solution(11296015810722087793)
XLA Ops:
  3.4 4.4 sort.31
  7.8 3.8 sort.32
  13.5 2.3 gather_fusion
  15.8 8.7 %ragged-dot-none.5 = f32[512,512]{1,0:T(8,128)} custom-call(s32[1]{0:T(128)} %get-tuple-element.27, s32[4]{0:T(128)} %get-tuple-element.28, s32[4]{0:T(128)} %get-tuple-element.29, s32[4]{0:T(128)} %get-tuple-element.30, s32[1]{0:T(128)} %get-tuple-element.27, f32[512,512]{1,0:T(8,128)} %gather_fusion, f32[3,512,512]{2,1,0:T(8,128)} %param.17), custom_call_target="tpu_custom_call" | custom-call | flops 268435456 | bytes 5242892 | tf_op jit(solution)/shard_map/ragged_dot_general/ragged-dot-none
  24.6 3.3 gather_fusion.1
  29.4 3.1 collective-permute-start
  38.5 3.4 collective-permute-start.2
  50.5 33.6 %psum.84 = f32[]{:T(128)} all-reduce(f32[]{:T(128)} %multiply_reduce_fusion.2), channel_id=1, replica_groups=mesh['parts'=2,'warp'=4,'weft'=2,'ply'=2] {'warp','weft','ply'}, use_global_device_ids=true, to_apply=%region_4.5 | all-reduce | flops 1 | bytes 8 | tf_op jit(solution)/shard_map/psum | solution.py:128
  87.1 14.7 %scatter_custom_fusion = f32[129]{0:T(256)S(1)} fusion(s32[2048]{0:T(1024)S(1)} %bitcast.138, f32[2048]{0:T(1024)S(1)} %bitcast.142, f32[]{:T(128)} %constant.17.clone.1), kind=kCustom, calls=%fused_computation.187 | custom fusion | flops 2048 | bytes 520 | tf_op jit(solution)/shard_map/scatter-add | solution.py:134
  101.8 5.8 psum.85
  107.6 8.4 %psum.86 = f32[128]{0:T(128)S(1)} all-reduce(f32[128]{0:T(128)S(1)} %psum.85), channel_id=1, replica_groups=mesh['parts'=2,'warp'=4,'weft'=2,'ply'=2] {'warp'}, use_global_device_ids=true, to_apply=%region_8.9 | all-reduce | flops 128 | bytes 1024 | tf_op jit(solution)/shard_map/psum | solution.py:137
  116.3 29.5 %all-reduce = f32[128]{0:T(128)S(1)} all-reduce(f32[128]{0:T(128)S(1)} %dynamic-update-slice), channel_id=1, replica_groups=mesh['parts'=2,'warp'=4,'weft'=2,'ply'=2] {'warp','weft','ply'}, use_global_device_ids=true, to_apply=%add | all-reduce | flops 128 | bytes 1024
  145.7 12.6 %gather_fusion.4 = f32[2048]{0:T(1024)S(1)} fusion(f32[128]{0:T(128)S(1)} %all-reduce, s32[2048]{0:T(1024)S(1)} %broadcast_clamp_fusion), kind=kCustom, calls=%fused_computation.4 | custom fusion | bytes 24576 | tf_op jit(solution)/shard_map/gather | solution.py:144
  158.4 2.3 gather_fusion.2
  160.7 8.7 %ragged-dot-none.4 = f32[512,512]{1,0:T(8,128)} custom-call(s32[1]{0:T(128)} %get-tuple-element.27, s32[4]{0:T(128)} %get-tuple-element.28, s32[4]{0:T(128)} %get-tuple-element.29, s32[4]{0:T(128)} %get-tuple-element.30, s32[1]{0:T(128)} %get-tuple-element.27, f32[512,512]{1,0:T(8,128)} %gather_fusion.2, f32[3,512,512]{2,1,0:T(8,128)} %param.16), custom_call_target="tpu_custom_call" | custom-call | flops 268435456 | bytes 5242892 | tf_op jit(solution)/shard_map/ragged_dot_general/ragged-dot-none
  169.4 3.9 gather_fusion.3
  183.7 4.0 collective-permute-done.7
  189.7 32.0 %psum.87 = f32[]{:T(128)} all-reduce(f32[]{:T(128)} %fusion.23), channel_id=1, replica_groups=mesh['parts'=2,'warp'=4,'weft'=2,'ply'=2] {'warp','weft','ply'}, use_global_device_ids=true, to_apply=%region_10.11 | all-reduce | flops 1 | bytes 8 | tf_op jit(solution)/shard_map/psum | solution.py:149
  224.7 2.3 gather_fusion.5
  227.0 8.7 %ragged-dot-none.3 = f32[512,512]{1,0:T(8,128)} custom-call(s32[1]{0:T(128)} %get-tuple-element.27, s32[4]{0:T(128)} %get-tuple-element.28, s32[4]{0:T(128)} %get-tuple-element.29, s32[4]{0:T(128)} %get-tuple-element.30, s32[1]{0:T(128)} %get-tuple-element.27, f32[512,512]{1,0:T(8,128)} %gather_fusion.5, f32[3,512,512]{2,1,0:T(8,128)} %param.17), custom_call_target="tpu_custom_call" | custom-call | flops 268435456 | bytes 5242892 | tf_op jit(solution)/shard_map/ragged_dot_general/ragged-dot-none
  235.8 3.9 gather_fusion.6
  248.4 4.1 collective-permute-done.11
  254.6 30.7 %psum.88 = f32[]{:T(128)} all-reduce(f32[]{:T(128)} %multiply_reduce_fusion.1), channel_id=1, replica_groups=mesh['parts'=2,'warp'=4,'weft'=2,'ply'=2] {'warp','weft','ply'}, use_global_device_ids=true, to_apply=%region_12.13 | all-reduce | flops 1 | bytes 8 | tf_op jit(solution)/shard_map/psum | solution.py:128
  289.1 14.7 %scatter_custom_fusion.1 = f32[129]{0:T(256)S(1)} fusion(s32[2048]{0:T(1024)S(1)} %bitcast.139, f32[2048]{0:T(1024)S(1)} %bitcast.143, f32[]{:T(128)} %constant.17.clone.1), kind=kCustom, calls=%fused_computation.185 | custom fusion | flops 2048 | bytes 520 | tf_op jit(solution)/shard_map/scatter-add | solution.py:134
  303.8 5.8 psum.89
  309.5 8.4 %psum.90 = f32[128]{0:T(128)S(1)} all-reduce(f32[128]{0:T(128)S(1)} %psum.89), channel_id=1, replica_groups=mesh['parts'=2,'warp'=4,'weft'=2,'ply'=2] {'warp'}, use_global_device_ids=true, to_apply=%region_16.17 | all-reduce | flops 128 | bytes 1024 | tf_op jit(solution)/shard_map/psum | solution.py:137
  318.2 29.5 %all-reduce.1 = f32[128]{0:T(128)S(1)} all-reduce(f32[128]{0:T(128)S(1)} %dynamic-update-slice.1), channel_id=1, replica_groups=mesh['parts'=2,'warp'=4,'weft'=2,'ply'=2] {'warp','weft','ply'}, use_global_device_ids=true, to_apply=%add.1 | all-reduce | flops 128 | bytes 1024
  347.7 12.6 %gather_fusion.9 = f32[2048]{0:T(1024)S(1)} fusion(f32[128]{0:T(128)S(1)} %all-reduce.1, s32[2048]{0:T(1024)S(1)} %broadcast_clamp_fusion), kind=kCustom, calls=%fused_computation.9 | custom fusion | bytes 24576 | tf_op jit(solution)/shard_map/gather | solution.py:144
  360.3 2.3 gather_fusion.7
  362.6 8.7 %ragged-dot-none.2 = f32[512,512]{1,0:T(8,128)} custom-call(s32[1]{0:T(128)} %get-tuple-element.27, s32[4]{0:T(128)} %get-tuple-element.28, s32[4]{0:T(128)} %get-tuple-element.29, s32[4]{0:T(128)} %get-tuple-element.30, s32[1]{0:T(128)} %get-tuple-element.27, f32[512,512]{1,0:T(8,128)} %gather_fusion.7, f32[3,512,512]{2,1,0:T(8,128)} %param.16), custom_call_target="tpu_custom_call" | custom-call | flops 268435456 | bytes 5242892 | tf_op jit(solution)/shard_map/ragged_dot_general/ragged-dot-none
  371.4 3.9 gather_fusion.8
  385.5 4.1 collective-permute-done.15
  391.6 32.2 %psum.91 = f32[]{:T(128)} all-reduce(f32[]{:T(128)} %fusion.22), channel_id=1, replica_groups=mesh['parts'=2,'warp'=4,'weft'=2,'ply'=2] {'warp','weft','ply'}, use_global_device_ids=true, to_apply=%region_18.19 | all-reduce | flops 1 | bytes 8 | tf_op jit(solution)/shard_map/psum | solution.py:149
  425.2 3.4 fusion.11
  430.9 8.7 %ragged-dot-none.1 = f32[512,512]{1,0:T(8,128)} custom-call(s32[1]{0:T(128)} %get-tuple-element.27, s32[4]{0:T(128)} %get-tuple-element.28, s32[4]{0:T(128)} %get-tuple-element.29, s32[4]{0:T(128)} %get-tuple-element.30, s32[1]{0:T(128)} %get-tuple-element.27, f32[512,512]{1,0:T(8,128)} %gather_fusion.10, f32[3,512,512]{2,1,0:T(8,128)} %param.17), custom_call_target="tpu_custom_call" | custom-call | flops 268435456 | bytes 5242892 | tf_op jit(solution)/shard_map/ragged_dot_general/ragged-dot-none
  439.6 3.2 gather_fusion.11
  452.5 3.1 collective-permute-done.19
  457.7 30.6 %psum.92 = f32[]{:T(128)} all-reduce(f32[]{:T(128)} %multiply_reduce_fusion), channel_id=1, replica_groups=mesh['parts'=2,'warp'=4,'weft'=2,'ply'=2] {'warp','weft','ply'}, use_global_device_ids=true, to_apply=%region_20.21 | all-reduce | flops 1 | bytes 8 | tf_op jit(solution)/shard_map/psum | solution.py:128
  492.4 14.7 %scatter_custom_fusion.2 = f32[129]{0:T(256)S(1)} fusion(s32[2048]{0:T(1024)S(1)} %bitcast.140, f32[2048]{0:T(1024)S(1)} %bitcast.141, f32[]{:T(128)} %constant.17.clone.1), kind=kCustom, calls=%fused_computation.183 | custom fusion | flops 2048 | bytes 520 | tf_op jit(solution)/shard_map/scatter-add | solution.py:134
  507.1 5.8 psum.93
  512.8 8.4 %psum.94 = f32[128]{0:T(128)S(1)} all-reduce(f32[128]{0:T(128)S(1)} %psum.93), channel_id=1, replica_groups=mesh['parts'=2,'warp'=4,'weft'=2,'ply'=2] {'warp'}, use_global_device_ids=true, to_apply=%region_24.25 | all-reduce | flops 128 | bytes 1024 | tf_op jit(solution)/shard_map/psum | solution.py:137
  521.5 29.5 %all-reduce.2 = f32[128]{0:T(128)S(1)} all-reduce(f32[128]{0:T(128)S(1)} %dynamic-update-slice.2), channel_id=1, replica_groups=mesh['parts'=2,'warp'=4,'weft'=2,'ply'=2] {'warp','weft','ply'}, use_global_device_ids=true, to_apply=%add.2 | all-reduce | flops 128 | bytes 1024
  551.0 12.6 %gather_fusion.14 = f32[2048]{0:T(1024)S(1)} fusion(f32[128]{0:T(128)S(1)} %all-reduce.2, s32[2048]{0:T(1024)S(1)} %broadcast_clamp_fusion), kind=kCustom, calls=%fused_computation.14 | custom fusion | bytes 24576 | tf_op jit(solution)/shard_map/gather | solution.py:144
  565.9 8.7 %ragged-dot-none = f32[512,512]{1,0:T(8,128)} custom-call(s32[1]{0:T(128)} %get-tuple-element.27, s32[4]{0:T(128)} %get-tuple-element.28, s32[4]{0:T(128)} %get-tuple-element.29, s32[4]{0:T(128)} %get-tuple-element.30, s32[1]{0:T(128)} %get-tuple-element.27, f32[512,512]{1,0:T(8,128)} %gather_fusion.12, f32[3,512,512]{2,1,0:T(8,128)} %param.16), custom_call_target="tpu_custom_call" | custom-call | flops 268435456 | bytes 5242892 | tf_op jit(solution)/shard_map/ragged_dot_general/ragged-dot-none
  574.7 3.9 gather_fusion.13
  588.9 4.1 collective-permute-done.23
  595.2 32.1 %psum.95 = f32[]{:T(128)} all-reduce(f32[]{:T(128)} %fusion.21), channel_id=1, replica_groups=mesh['parts'=2,'warp'=4,'weft'=2,'ply'=2] {'warp','weft','ply'}, use_global_device_ids=true, to_apply=%region_26.27 | all-reduce | flops 1 | bytes 8 | tf_op jit(solution)/shard_map/psum | solution.py:149
  628.6 2.7 multiply_subtract_fusion
  (259 shorter events, 94.3 us)
Async XLA Ops:
  0.6 85.5 %copy-start = (f32[3,4,512]{2,1,0:T(4,128)S(1)}, f32[3,4,512]{2,1,0:T(4,128)}, u32[]{:S(2)}) copy-start(f32[3,4,512]{2,1,0:T(4,128)} %param.18) | copy-start | bytes 73732
  11.8 378.1 %copy-start.2 = (f32[4,128,128]{2,1,0:T(8,128)}, f32[4,128,128]{2,1,0:T(8,128)S(1)}, u32[]{:S(2)}) copy-start(f32[4,128,128]{2,1,0:T(8,128)S(1)} %broadcast_in_dim.140) | copy-start | bytes 786436
  11.9 378.0 %copy-start.5 = (f32[4,128,128]{2,1,0:T(8,128)}, f32[4,128,128]{2,1,0:T(8,128)S(1)}, u32[]{:S(2)}) copy-start(f32[4,128,128]{2,1,0:T(8,128)S(1)} %broadcast_in_dim.135) | copy-start | bytes 786436
  12.0 377.9 %copy-start.8 = (f32[4,128,128]{2,1,0:T(8,128)}, f32[4,128,128]{2,1,0:T(8,128)S(1)}, u32[]{:S(2)}) copy-start(f32[4,128,128]{2,1,0:T(8,128)S(1)} %broadcast_in_dim.138) | copy-start | bytes 786436
  24.6 9.3 %copy-start.41 = (s32[4,4,128]{2,1,0:T(4,128)S(1)}, s32[4,4,128]{2,1,0:T(4,128)}, u32[]{:S(2)}) copy-start(s32[4,4,128]{2,1,0:T(4,128)} %param.15) | copy-start | bytes 24580
  27.8 7.7 %copy-start.43 = (s32[4,128]{1,0:T(4,128)S(1)}, s32[4,128]{1,0:T(4,128)}, u32[]{:S(2)}) copy-start(s32[4,128]{1,0:T(4,128)} %param.14) | copy-start | bytes 6148
  27.8 16.0 %copy-start.44 = (u32[32]{0:T(128)S(1)}, u32[32]{0:T(128)}, u32[]{:S(2)}) copy-start(u32[32]{0:T(128)} %constant.48) | copy-start | bytes 388
  29.4 19.4 %copy-start.11 = (f32[4,128,512]{2,1,0:T(8,128)S(1)}, f32[4,128,512]{2,1,0:T(8,128)}, u32[]{:S(2)}) copy-start(f32[4,128,512]{2,1,0:T(8,128)} %param.11) | copy-start | bytes 3145732
  29.4 6.1 collective-permute-start
  32.5 5.1 collective-permute-start.1
  38.5 7.6 %collective-permute-start.2 = (f32[6,1,256]{2,1,0:T(1,128)S(1)}, f32[6,1,256]{2,1,0:T(1,128)S(1)}, u32[]{:S(2)}, u32[]{:S(2)}) collective-permute-start(f32[6,1,256]{2,1,0:T(1,128)S(1)} %get-tuple-element.103), channel_id=1, source_target_pairs={{0,2},{1,3},{4,6},{5,7},{8,10},{9,11},{12,14},{13,15},{16,18},{17,... | collective-permute-start | bytes 18440 | tf_op jit(solution)/shard_map/ppermute | solution.py:17
  41.9 5.5 collective-permute-start.3
  48.8 35.8 %copy-start.39 = (f32[4,128,512]{2,1,0:T(8,128)S(1)}, f32[4,128,512]{2,1,0:T(8,128)}, u32[]{:S(2)}) copy-start(f32[4,128,512]{2,1,0:T(8,128)} %param.12) | copy-start | bytes 3145732
  49.9 66.0 %copy-start.42 = (f32[8,128]{1,0:T(8,128)S(1)}, f32[8,128]{1,0:T(8,128)}, u32[]{:S(2)}) copy-start(f32[8,128]{1,0:T(8,128)} %param.19) | copy-start | bytes 12292
  175.8 3.1 collective-permute-start.4
  177.6 3.2 collective-permute-start.5
  180.9 2.8 collective-permute-start.6
  182.2 5.5 collective-permute-start.7
  187.9 36.8 %copy-start.16 = (f32[4,128,128]{2,1,0:T(8,128)}, f32[4,128,128]{2,1,0:T(8,128)S(1)}, u32[]{:S(2)}) copy-start(f32[4,128,128]{2,1,0:T(8,128)S(1)} %get-tuple-element.73) | copy-start | bytes 786436
  239.7 8.6 %copy-start.12 = (f32[512,512]{1,0:T(8,128)S(1)}, f32[512,512]{1,0:T(8,128)}, u32[]{:S(2)}) copy-start(f32[512,512]{1,0:T(8,128)} %gather_fusion.6) | copy-start | bytes 3145732
  241.2 3.7 collective-permute-start.8
  242.5 3.2 collective-permute-start.9
  245.7 2.7 collective-permute-start.10
  247.0 5.5 collective-permute-start.11
  377.8 3.1 collective-permute-start.12
  379.5 3.2 collective-permute-start.13
  382.8 2.7 collective-permute-start.14
  384.1 5.5 collective-permute-start.15
  389.8 34.0 %copy-start.35 = (f32[4,128,128]{2,1,0:T(8,128)}, f32[4,128,128]{2,1,0:T(8,128)S(1)}, u32[]{:S(2)}) copy-start(f32[4,128,128]{2,1,0:T(8,128)S(1)} %get-tuple-element.53) | copy-start | bytes 786436
  443.9 11.7 %copy-start.14 = (f32[512,512]{1,0:T(8,128)S(1)}, f32[512,512]{1,0:T(8,128)}, u32[]{:S(2)}) copy-start(f32[512,512]{1,0:T(8,128)} %copy-done.13) | copy-start | bytes 3145732
  443.9 12.8 %copy-start.3 = (f32[4,128,128]{2,1,0:T(8,128)S(1)}, f32[4,128,128]{2,1,0:T(8,128)}, u32[]{:S(2)}) copy-start(f32[4,128,128]{2,1,0:T(8,128)} %copy-done.2) | copy-start | bytes 786436
  443.9 12.7 %copy-start.6 = (f32[4,128,128]{2,1,0:T(8,128)S(1)}, f32[4,128,128]{2,1,0:T(8,128)}, u32[]{:S(2)}) copy-start(f32[4,128,128]{2,1,0:T(8,128)} %copy-done.5) | copy-start | bytes 786436
  443.9 12.7 %copy-start.9 = (f32[4,128,128]{2,1,0:T(8,128)S(1)}, f32[4,128,128]{2,1,0:T(8,128)}, u32[]{:S(2)}) copy-start(f32[4,128,128]{2,1,0:T(8,128)} %copy-done.8) | copy-start | bytes 786436
  443.9 12.7 %copy-start.15 = (f32[4,128,512]{2,1,0:T(8,128)S(1)}, f32[4,128,512]{2,1,0:T(8,128)}, u32[]{:S(2)}) copy-start(f32[4,128,512]{2,1,0:T(8,128)} %get-tuple-element.32) | copy-start | bytes 3145732
  443.9 3.9 collective-permute-start.16
  445.5 3.2 collective-permute-start.17
  448.8 3.7 collective-permute-start.18
  450.1 5.5 collective-permute-start.19
  455.8 32.5 %copy-start.27 = (f32[4,128,128]{2,1,0:T(8,128)}, f32[4,128,128]{2,1,0:T(8,128)S(1)}, u32[]{:S(2)}) copy-start(f32[4,128,128]{2,1,0:T(8,128)S(1)} %get-tuple-element.43) | copy-start | bytes 786436
  491.3 140.0 %copy-start.1 = (f32[4,128,512]{2,1,0:T(8,128)}, f32[4,128,512]{2,1,0:T(8,128)S(1)}, u32[]{:S(2)}) copy-start(f32[4,128,512]{2,1,0:T(8,128)S(1)} %multiply_add_fusion.1) | copy-start | bytes 3145732
  581.1 13.2 %copy-start.4 = (f32[4,128,128]{2,1,0:T(8,128)S(1)}, f32[4,128,128]{2,1,0:T(8,128)}, u32[]{:S(2)}) copy-start(f32[4,128,128]{2,1,0:T(8,128)} %copy-done.2) | copy-start | bytes 786436
  581.1 13.2 %copy-start.7 = (f32[4,128,128]{2,1,0:T(8,128)S(1)}, f32[4,128,128]{2,1,0:T(8,128)}, u32[]{:S(2)}) copy-start(f32[4,128,128]{2,1,0:T(8,128)} %copy-done.5) | copy-start | bytes 786436
  581.1 13.1 %copy-start.10 = (f32[4,128,128]{2,1,0:T(8,128)S(1)}, f32[4,128,128]{2,1,0:T(8,128)}, u32[]{:S(2)}) copy-start(f32[4,128,128]{2,1,0:T(8,128)} %copy-done.8) | copy-start | bytes 786436
  581.1 3.3 collective-permute-start.20
  583.0 3.2 collective-permute-start.21
  586.3 2.7 collective-permute-start.22
  587.5 5.5 collective-permute-start.23
  628.6 2.8 copy-start.40
  (21 other events, 17.4 us)
